TPU v7x, 32 devices: a whole 2x2x4 slice. The times are simulated.
32 devices in a mesh: dp: 4 (over y, x), fsdp: 8 (over z, core).
Axes of the slice: x: 2, y: 2, z: 4, core: 2. Of those that a mesh axis runs over, the one named last changes fastest.
Arguments:
- inputs: bfloat16 [32, 512, 768], P(('dp', 'fsdp')), may hold values from -6 to 6
- seg_ids: int32 [32, 512], P(('dp', 'fsdp')), may hold values from 0 to 7, never falling along the last dimension, each value on 1 to 128 neighbouring positions
- pool_index: int32 [32, 8], P(('dp', 'fsdp')), may hold values from 0 to 7, each once within a row
- w_query: bfloat16 [768, 768], P('fsdp'), may hold values from -0.109375 to 0.109375
- w_key: bfloat16 [768, 768], P('fsdp'), may hold values from -0.109375 to 0.109375
- w_value: bfloat16 [768, 768], P('fsdp'), may hold values from -0.21875 to 0.21875
- w_out: bfloat16 [768, 768], P('fsdp'), may hold values from -0.625 to 0.625
- w_up: bfloat16 [768, 3072], P('fsdp'), may hold values from -0.21875 to 0.21875
- w_down: bfloat16 [3072, 768], P('fsdp'), may hold values from -0.109375 to 0.109375
- w_proj: bfloat16 [768, 768], P('fsdp'), may hold values from -0.21875 to 0.21875
- gain_attn: float32 [768], replicated, may hold values from 0.5 to 1.5
- gain_ffn: float32 [768], replicated, may hold values from 0.5 to 1.5
- gain_final: float32 [768], replicated, may hold values from 0.5 to 1.5
- bias_table: float32 [32, 12], replicated, may hold values from -4 to 4
- emb_grad: float32 [32, 8, 768], P(('dp', 'fsdp')), may hold values from -6 to 6
Outputs:
- embeddings: float32 [32, 8, 768], P(('dp', 'fsdp'))
- input_grad: float32 [32, 512, 768], P(('dp', 'fsdp'))
- grad_query: float32 [768, 768], P('fsdp')
- grad_key: float32 [768, 768], P('fsdp')
- grad_value: float32 [768, 768], P('fsdp')
- grad_out: float32 [768, 768], P('fsdp')
- grad_up: float32 [768, 3072], P('fsdp')
- grad_down: float32 [3072, 768], P('fsdp')
- grad_proj: float32 [768, 768], P('fsdp')
- grad_gain_attn: float32 [768], replicated
- grad_gain_ffn: float32 [768], replicated
- grad_gain_final: float32 [768], replicated
- grad_table: float32 [32, 12], replicated
Inputs may be any that keep to these rules, and one draw needn't show every extreme that they name: `seg_ids`: within a row the ids never fall, and each of 0 to 7 holds 1 to 128 tokens. `pool_index`: each row is a permutation of 0 to 7.
All inputs are finite; a program needn't handle non-finite values.
Results may differ from a plain program's by a relative error of at most 0.015.
Values may be sent and summed in bfloat16 or wider, within the bound.
A program may use at most 192 MiB of HBM per device.

v0:
```python
from functools import partial

import jax
import jax.numpy as jnp
import numpy as np
from jax import lax
from jax.sharding import PartitionSpec as P

REACH = 128


EPSILON = 1e-06
HIGH = lax.Precision.HIGHEST


def bucket_table(length, buckets, reach):
    positions = np.arange(length)
    relative = positions[None, :] - positions[:, None]
    halfway = buckets // 2
    exact_span = halfway // 2
    distance = np.abs(relative)
    logged = exact_span + (
        np.log(np.maximum(distance, 1) / exact_span)
        / np.log(reach / exact_span)
        * (halfway - exact_span)
    ).astype(np.int64)
    logged = np.minimum(logged, halfway - 1)
    result = (relative > 0).astype(np.int64) * halfway + np.where(
        distance < exact_span, distance, logged
    )
    return result.astype(np.int32)


def rms_forward(values, gain):
    factor = lax.rsqrt(jnp.mean(values * values, axis=-1, keepdims=True) + EPSILON)
    return (values * factor * gain, factor)


def rms_backward(values, factor, gain, upstream):
    normed = values * factor
    gain_grad = jnp.sum(upstream * normed, axis=0)
    inner = upstream * gain
    return (factor * (inner - normed * jnp.mean(inner * normed, axis=-1, keepdims=True)), gain_grad)


def matmul(left, right):
    return jnp.dot(left, right, preferred_element_type=jnp.float32)


def matmul_left(left, right):
    return lax.dot_general(
        left, right, (((0,), (0,)), ((), ())), preferred_element_type=jnp.float32
    )


def matmul_right(left, right):
    return lax.dot_general(
        left, right, (((1,), (1,)), ((), ())), preferred_element_type=jnp.float32
    )


def row_scores(query_row, key_row, seg_row, bias):
    raw_scores = jnp.einsum("qhd,khd->hqk", query_row, key_row, preferred_element_type=jnp.float32)
    same_doc = (seg_row[:, None] == seg_row[None, :])[None]
    return jnp.where(same_doc, raw_scores + bias, -1e30)


def per_device(
    inputs,
    seg_ids,
    pool_index,
    w_query,
    w_key,
    w_value,
    w_out,
    w_up,
    w_down,
    w_proj,
    gain_attn,
    gain_ffn,
    gain_final,
    bias_table,
    emb_grad,
):
    rows, length, width = inputs.shape
    buckets, heads = bias_table.shape
    head_dim = width // heads
    tokens = rows * length
    head_shape = (rows, length, heads, head_dim)
    gathered = (
        lax.all_gather(w_query, "fsdp", axis=0, tiled=True),
        lax.all_gather(w_key, "fsdp", axis=0, tiled=True),
        lax.all_gather(w_value, "fsdp", axis=0, tiled=True),
        lax.all_gather(w_out, "fsdp", axis=0, tiled=True),
        lax.all_gather(w_up, "fsdp", axis=0, tiled=True),
        lax.all_gather(w_down, "fsdp", axis=0, tiled=True),
        lax.all_gather(w_proj, "fsdp", axis=0, tiled=True),
    )
    full_query, full_key, full_value, full_out, full_up, full_down, full_proj = gathered
    flat = inputs.reshape(tokens, width).astype(jnp.float32)
    normed_one, factor_one = rms_forward(flat, gain_attn)
    normed_one = normed_one.astype(jnp.bfloat16)
    queries = matmul(normed_one, full_query).astype(jnp.bfloat16).reshape(head_shape)
    key_rows = matmul(normed_one, full_key).astype(jnp.bfloat16).reshape(head_shape)
    value_rows = matmul(normed_one, full_value).astype(jnp.bfloat16).reshape(head_shape)
    bucket_ids = jnp.asarray(bucket_table(length, buckets, REACH))
    onehot_cols = (
        jnp.arange(buckets, dtype=jnp.int32)[:, None] == bucket_ids.reshape(1, length * length)
    ).astype(jnp.bfloat16)
    bias = jnp.dot(bias_table.T, onehot_cols.astype(jnp.float32), precision=HIGH).reshape(
        heads, length, length
    )

    def attend_row(pieces):
        query_row, key_row, value_row, seg_row = pieces
        scores = row_scores(query_row, key_row, seg_row, bias)
        row_peak = jnp.max(scores, axis=-1, keepdims=True)
        log_total = row_peak + jnp.log(jnp.sum(jnp.exp(scores - row_peak), axis=-1, keepdims=True))
        soft_low = jnp.exp(scores - log_total).astype(jnp.bfloat16)
        mixed = jnp.einsum("hqk,khd->qhd", soft_low, value_row, preferred_element_type=jnp.float32)
        return (mixed.astype(jnp.bfloat16), log_total)

    attended, log_totals = lax.map(attend_row, (queries, key_rows, value_rows, seg_ids))
    attended_flat = attended.reshape(tokens, width)
    hidden_one = flat + matmul(attended_flat, full_out)
    normed_two, factor_two = rms_forward(hidden_one, gain_ffn)
    normed_two = normed_two.astype(jnp.bfloat16)
    pre_act = matmul(normed_two, full_up)
    activated = jax.nn.gelu(pre_act, approximate=True).astype(jnp.bfloat16)
    hidden_two = hidden_one + matmul(activated, full_down)
    final_rows, factor_three = rms_forward(hidden_two, gain_final)
    member = (seg_ids[:, None, :] == pool_index[:, :, None]).astype(jnp.float32)
    counts = jnp.sum(member, axis=-1, keepdims=True)
    pooled = (
        jnp.einsum("rpl,rld->rpd", member, final_rows.reshape(rows, length, width), precision=HIGH)
        / counts
    )
    proj_full = full_proj.astype(jnp.float32)
    projected = jnp.einsum("rpd,de->rpe", pooled, proj_full, precision=HIGH)
    inverse_len = lax.rsqrt(jnp.sum(projected * projected, axis=-1, keepdims=True) + EPSILON)
    embeddings = projected * inverse_len
    emb_dot = jnp.sum(emb_grad * embeddings, axis=-1, keepdims=True)
    projected_grad = inverse_len * (emb_grad - embeddings * emb_dot)
    grad_proj = jnp.einsum("rpd,rpe->de", pooled, projected_grad, precision=HIGH)
    pooled_grad = jnp.einsum("rpe,de->rpd", projected_grad, proj_full, precision=HIGH) / counts
    final_grad = jnp.einsum("rpl,rpd->rld", member, pooled_grad, precision=HIGH).reshape(
        tokens, width
    )
    stream_two, grad_gain_final = rms_backward(hidden_two, factor_three, gain_final, final_grad)
    back_weights = (
        lax.all_gather(w_query, "fsdp", axis=0, tiled=True),
        lax.all_gather(w_key, "fsdp", axis=0, tiled=True),
        lax.all_gather(w_value, "fsdp", axis=0, tiled=True),
        lax.all_gather(w_out, "fsdp", axis=0, tiled=True),
        lax.all_gather(w_up, "fsdp", axis=0, tiled=True),
        lax.all_gather(w_down, "fsdp", axis=0, tiled=True),
        lax.all_gather(w_proj, "fsdp", axis=0, tiled=True),
    )
    back_query, back_key, back_value, back_out, back_up, back_down, back_proj = back_weights
    ffn_grad = stream_two.astype(jnp.bfloat16)
    grad_down = matmul_left(activated, ffn_grad)
    act_grad = matmul_right(ffn_grad, back_down)
    gelu_pullback = jax.vjp(partial(jax.nn.gelu, approximate=True), pre_act)[1]
    pre_grad = gelu_pullback(act_grad)[0].astype(jnp.bfloat16)
    grad_up = matmul_left(normed_two, pre_grad)
    normed_two_grad = matmul_right(pre_grad, back_up)
    stream_mid, grad_gain_ffn = rms_backward(hidden_one, factor_two, gain_ffn, normed_two_grad)
    stream_one = stream_two + stream_mid
    attn_grad = stream_one.astype(jnp.bfloat16)
    grad_out = matmul_left(attended_flat, attn_grad)
    mixed_grad = matmul_right(attn_grad, back_out).astype(jnp.bfloat16).reshape(head_shape)

    def attend_back(pieces):
        query_row, key_row, value_row, seg_row, log_total, upstream_row = pieces
        scores = row_scores(query_row, key_row, seg_row, bias)
        soft_rows = jnp.exp(scores - log_total)
        soft_grad = jnp.einsum(
            "qhd,khd->hqk", upstream_row, value_row, preferred_element_type=jnp.float32
        )
        score_grad = (
            soft_rows * (soft_grad - jnp.sum(soft_rows * soft_grad, axis=-1, keepdims=True))
        ).astype(jnp.bfloat16)
        query_grad = jnp.einsum(
            "hqk,khd->qhd", score_grad, key_row, preferred_element_type=jnp.float32
        ).astype(jnp.bfloat16)
        key_grad = jnp.einsum(
            "hqk,qhd->khd", score_grad, query_row, preferred_element_type=jnp.float32
        ).astype(jnp.bfloat16)
        value_grad = jnp.einsum(
            "hqk,qhd->khd",
            soft_rows.astype(jnp.bfloat16),
            upstream_row,
            preferred_element_type=jnp.float32,
        ).astype(jnp.bfloat16)
        table_grad = matmul_right(score_grad.reshape(heads, length * length), onehot_cols)
        return (query_grad, key_grad, value_grad, table_grad)

    query_grads, key_grads, value_grads, table_grads = lax.map(
        attend_back, (queries, key_rows, value_rows, seg_ids, log_totals, mixed_grad)
    )
    grad_table = jnp.sum(table_grads, axis=0).T
    query_flat = query_grads.reshape(tokens, width)
    key_flat = key_grads.reshape(tokens, width)
    value_flat = value_grads.reshape(tokens, width)
    grad_query = matmul_left(normed_one, query_flat)
    grad_key = matmul_left(normed_one, key_flat)
    grad_value = matmul_left(normed_one, value_flat)
    normed_one_grad = (
        matmul_right(query_flat, back_query)
        + matmul_right(key_flat, back_key)
        + matmul_right(value_flat, back_value)
    )
    stream_in, grad_gain_attn = rms_backward(flat, factor_one, gain_attn, normed_one_grad)
    input_grad = (stream_one + stream_in).reshape(rows, length, width)
    shard_query, shard_key, shard_value, shard_out, shard_up, shard_down, shard_proj = (
        lax.psum_scatter(grad_query, "fsdp", scatter_dimension=0, tiled=True),
        lax.psum_scatter(grad_key, "fsdp", scatter_dimension=0, tiled=True),
        lax.psum_scatter(grad_value, "fsdp", scatter_dimension=0, tiled=True),
        lax.psum_scatter(grad_out, "fsdp", scatter_dimension=0, tiled=True),
        lax.psum_scatter(grad_up, "fsdp", scatter_dimension=0, tiled=True),
        lax.psum_scatter(grad_down, "fsdp", scatter_dimension=0, tiled=True),
        lax.psum_scatter(grad_proj, "fsdp", scatter_dimension=0, tiled=True),
    )
    summed = (
        lax.psum(shard_query.astype(jnp.bfloat16), "dp").astype(jnp.float32),
        lax.psum(shard_key.astype(jnp.bfloat16), "dp").astype(jnp.float32),
        lax.psum(shard_value.astype(jnp.bfloat16), "dp").astype(jnp.float32),
        lax.psum(shard_out.astype(jnp.bfloat16), "dp").astype(jnp.float32),
        lax.psum(shard_up.astype(jnp.bfloat16), "dp").astype(jnp.float32),
        lax.psum(shard_down.astype(jnp.bfloat16), "dp").astype(jnp.float32),
        lax.psum(shard_proj.astype(jnp.bfloat16), "dp").astype(jnp.float32),
    )
    smalls = lax.psum((grad_gain_attn, grad_gain_ffn, grad_gain_final, grad_table), ("dp", "fsdp"))
    return (
        embeddings,
        input_grad,
        summed[0],
        summed[1],
        summed[2],
        summed[3],
        summed[4],
        summed[5],
        summed[6],
        smalls[0],
        smalls[1],
        smalls[2],
        smalls[3],
    )


def solution(mesh):
    return jax.shard_map(
        per_device,
        mesh=mesh,
        in_specs=(
            P(("dp", "fsdp"), None, None),
            P(("dp", "fsdp"), None),
            P(("dp", "fsdp"), None),
            P("fsdp", None),
            P("fsdp", None),
            P("fsdp", None),
            P("fsdp", None),
            P("fsdp", None),
            P("fsdp", None),
            P("fsdp", None),
            P(),
            P(),
            P(),
            P(),
            P(("dp", "fsdp"), None, None),
        ),
        out_specs=(
            P(("dp", "fsdp"), None, None),
            P(("dp", "fsdp"), None, None),
            P("fsdp", None),
            P("fsdp", None),
            P("fsdp", None),
            P("fsdp", None),
            P("fsdp", None),
            P("fsdp", None),
            P("fsdp", None),
            P(),
            P(),
            P(),
            P(),
        ),
        check_vma=False,
    )
```

profile of v0, /device:TPU:12, one launch (start us, length us, event | category | flops | bytes accessed | tf_op | source)
XLA Modules:
  0.0 750.2 jit_solution(3709220912776733040)
XLA Ops:
  12.7 11.5 %fusion.1 = f32[262144,12]{0,1:T(8,128)S(1)} fusion(f32[32,12]{0,1:T(8,128)S(1)} %copy-done, s32[262144]{0:T(1024)S(1)} %copy-done.20), kind=kOutput, calls=%fused_computation.2 | convolution fusion | flops 1216348160 | bytes 13633024 | tf_op jit(solution)/shard_map/dot_general | solution.py:110
  24.2 19.1 %copy.65 = f32[2,8,512,512]{3,2,1,0:T(8,128)} copy(f32[2,8,512,512]{3,1,2,0:T(8,128)S(1)} %bitcast.124) | data formatting | bytes 33554432
  43.3 10.6 %slice = f32[12,512,512]{2,1,0:T(8,128)} slice(f32[16,512,512]{2,1,0:T(8,128)} %bitcast.125), slice={[0:12], [0:512], [0:512]} | slice | bytes 25165824 | tf_op jit(solution)/shard_map/reshape | solution.py:110
  54.0 12.8 %copy.54 = f32[12,512,512]{1,2,0:T(8,128)} copy(f32[12,512,512]{2,1,0:T(8,128)} %slice) | data formatting | bytes 25165824 | tf_op jit(solution)/shard_map/reshape | solution.py:110
  71.7 10.0 %all-gather.8.cloned.1.call-done = bf16[768,768]{1,0:T(8,128)(2,1)} async-done(((bf16[96,768]{1,0:T(8,128)(2,1)}), bf16[768,768]{1,0:T(8,128)(2,1)}) %all-gather.8.cloned.1.call-update) | async-done | bytes 1179664 | tf_op jit(solution)/shard_map/all_gather | solution.py:93
  86.2 6.5 fusion.81
  100.1 5.5 all-gather.14.cloned.1.call-done
  108.1 49.0 %all-gather.16.cloned.1.call-done = bf16[768,3072]{1,0:T(8,128)(2,1)} async-done(((bf16[96,3072]{1,0:T(8,128)(2,1)}), bf16[768,3072]{1,0:T(8,128)(2,1)}) %all-gather.16.cloned.1.call-update) | async-done | bytes 4718608 | tf_op jit(solution)/shard_map/all_gather | solution.py:95
  157.2 7.3 fusion.71
  164.5 44.7 %all-gather.18.cloned.1.call-done = bf16[3072,768]{1,0:T(8,128)(2,1)} async-done(((bf16[384,768]{1,0:T(8,128)(2,1)}), bf16[3072,768]{1,0:T(8,128)(2,1)}) %all-gather.18.cloned.1.call-update) | async-done | bytes 4718608 | tf_op jit(solution)/shard_map/all_gather | solution.py:96
  209.2 8.5 %multiply_reduce_fusion.5 = (f32[512]{0:T(512)S(1)}, f32[512,768]{1,0:T(8,128)S(1)}) fusion(f32[512,768]{1,0:T(8,128)} %copy-done.5, bf16[3072,768]{1,0:T(8,128)(2,1)} %all-gather.18.cloned.1.call-done, f32[512,3072]{1,0:T(8,128)} %fusion.71), kind=kOutput, calls=%fused_computation.51 | convolution fusion | flops 2431254016 | bytes 14157824 | tf_op jit(solution)/shard_map/dot_general | solution.py:47
  218.5 15.4 %all-gather.20.cloned.1.call-done = bf16[768,768]{1,0:T(8,128)(2,1)} async-done(((bf16[96,768]{1,0:T(8,128)(2,1)}), bf16[768,768]{1,0:T(8,128)(2,1)}) %all-gather.20.cloned.1.call-update) | async-done | bytes 1179664 | tf_op jit(solution)/shard_map/all_gather | solution.py:97
  240.8 8.7 %fusion.11 = bf16[512,3072]{1,0:T(8,128)(2,1)S(1)} fusion(f32[512,3072]{1,0:T(8,128)} %fusion.71, bf16[3072,768]{1,0:T(8,128)(2,1)S(1)} %bitcast.154, f32[512,768]{1,0:T(8,128)S(1)} %subtract_multiply_fusion), kind=kOutput, calls=%fused_computation.19 | convolution fusion | flops 2447769600 | bytes 15728640 | tf_op jit(solution)/shard_map/dot_general | solution.py:57
  249.5 3.3 multiply_reduce_fusion.2
  256.3 3.5 fusion.57
  265.1 7.1 fusion.38
  275.6 8.0 %multiply_reduce_fusion = (f32[12,512]{1,0:T(8,128)S(1)}, f32[12,512,512]{1,2,0:T(8,128)S(1)}) fusion(f32[12,512,512]{1,2,0:T(8,128)} %copy-done.2, f32[12,512]{1,0:T(8,128)S(1)} %log_add_fusion, bf16[512,12,64]{0,2,1:T(8,128)(2,1)} %bitcast.133, bf16[512,12,64]{0,2,1:T(8,128)(2,1)} %bitcast.131), kind=kOutput, calls=%fused_computation.6 | convolution fusion | flops 412084224 | bytes 26787840 | tf_op jit(solution)/shard_map/while/body/eval_jaxpr/qhd,khd->hqk/dot_general | solution.py:177
  283.6 6.5 multiply_convert_fusion
  296.1 3.9 convolution_convert_fusion.5
  303.4 10.3 %fusion.51 = f32[3072,768]{1,0:T(8,128)} fusion(f32[512,768]{1,0:T(8,128)} %copy-done.14, f32[512,3072]{1,0:T(8,128)} %fusion.71), kind=kOutput, calls=%fused_computation.73 | convolution fusion | flops 2430468096 | bytes 17301504 | tf_op jit(solution)/shard_map/dot_general | solution.py:51
  313.7 8.8 %fusion.70 = f32[768,3072]{1,0:T(8,128)} fusion(bf16[512,3072]{1,0:T(8,128)(2,1)} %copy-done.16, f32[512,768]{1,0:T(8,128)} %copy-done.5, f32[768]{0:T(1024)S(1)} %copy-done.25, f32[512]{0:T(512)S(1)} %add_rsqrt_fusion.1), kind=kOutput, calls=%fused_computation.101 | convolution fusion | flops 2417098752 | bytes 14160896 | tf_op jit(solution)/shard_map/dot_general | solution.py:51
  330.2 34.4 %reduce-scatter.12.cloned.1.call-done = f32[96,768]{1,0:T(8,128)} async-done(((f32[768,768]{1,0:T(8,128)}), f32[96,768]{1,0:T(8,128)}) %reduce-scatter.12.cloned.1.call-update) | async-done | bytes 294928 | tf_op jit(solution)/shard_map/reduce_scatter | solution.py:218
  366.2 36.3 %reduce-scatter.10.cloned.1.call-done = f32[96,768]{1,0:T(8,128)} async-done(((f32[768,768]{1,0:T(8,128)}), f32[96,768]{1,0:T(8,128)}) %reduce-scatter.10.cloned.1.call-update) | async-done | bytes 294928 | tf_op jit(solution)/shard_map/reduce_scatter | solution.py:217
  404.2 36.1 %reduce-scatter.8.cloned.1.call-done = f32[96,768]{1,0:T(8,128)} async-done(((f32[768,768]{1,0:T(8,128)}), f32[96,768]{1,0:T(8,128)}) %reduce-scatter.8.cloned.1.call-update) | async-done | bytes 294928 | tf_op jit(solution)/shard_map/reduce_scatter | solution.py:216
  441.9 100.3 %reduce-scatter.18.cloned.1.call-done = f32[384,768]{1,0:T(8,128)} async-done(((f32[3072,768]{1,0:T(8,128)}), f32[384,768]{1,0:T(8,128)}) %reduce-scatter.18.cloned.1.call-update) | async-done | bytes 1179664 | tf_op jit(solution)/shard_map/reduce_scatter | solution.py:221
  544.3 97.9 %reduce-scatter.16.cloned.1.call-done = f32[96,3072]{1,0:T(8,128)} async-done(((f32[768,3072]{1,0:T(8,128)}), f32[96,3072]{1,0:T(8,128)}) %reduce-scatter.16.cloned.1.call-update) | async-done | bytes 1179664 | tf_op jit(solution)/shard_map/reduce_scatter | solution.py:220
  647.7 8.9 %copy.60 = bf16[12,512,512]{2,1,0:T(8,128)(2,1)} copy(bf16[12,512,512]{1,2,0:T(8,128)(2,1)} %copy-done.3) | data formatting | bytes 12582912 | tf_op jit(solution)/shard_map/while/body/eval_jaxpr/convert_element_type | solution.py:182
  656.6 6.7 pad
  663.3 11.6 %copy.66 = bf16[2,8,512,512]{3,1,2,0:T(8,128)(2,1)} copy(bf16[2,8,512,512]{3,2,1,0:T(8,128)(2,1)} %bitcast.126) | data formatting | bytes 16777216
  675.0 4.4 fusion.29
  679.4 7.7 %fusion = f32[32,12]{0,1:T(8,128)S(1)} fusion(bf16[12,262144]{1,0:T(8,128)(2,1)} %bitcast.129, s32[262144]{0:T(1024)S(1)} %copy-done.21), kind=kOutput, calls=%fused_computation.1 | convolution fusion | flops 209715200 | bytes 7341568 | tf_op jit(solution)/shard_map/while/body/eval_jaxpr/dot_general | solution.py:57
  687.1 43.5 %all-reduce = (f32[768]{0:T(1024)}, f32[768]{0:T(1024)}, f32[768]{0:T(1024)}, f32[32,12]{0,1:T(8,128)}) all-reduce(f32[768]{0:T(1024)S(1)} %get-tuple-element.67, f32[768]{0:T(1024)S(1)} %copy-done.33, f32[768]{0:T(1024)S(1)} %get-tuple-element.63, f32[32,12]{0,1:T(8,128)S(1)} %fusion), channel_id=1, replica_groups=mesh['dp'=4,'fsdp'=8] {'dp','fsdp'}, use_global_device_ids=true, to_apply=%region_27.28 | all-reduce | flops 2688 | bytes 21504 | tf_op jit(solution)/shard_map/psum | solution.py:233
  (164 shorter events, 86.5 us)
Async XLA Ops:
  7.2 59.6 %all-gather.12.cloned.1.call-start = ((), (), s32[]{:S(2)}) async-start(), calls=%async_computation.9 | async-start | bytes 1327104 | tf_op jit(solution)/shard_map/all_gather | solution.py:92
  8.0 61.3 %all-gather.10.cloned.1.call-start = ((), (), s32[]{:S(2)}) async-start(), calls=%async_computation.8 | async-start | bytes 1327104 | tf_op jit(solution)/shard_map/all_gather | solution.py:91
  8.7 73.0 %all-gather.8.cloned.1.call-start = ((), (), s32[]{:S(2)}) async-start(), calls=%async_computation.7 | async-start | bytes 1327104 | tf_op jit(solution)/shard_map/all_gather | solution.py:93
  9.5 96.2 %all-gather.14.cloned.1.call-start = ((), (), s32[]{:S(2)}) async-start(), calls=%async_computation.10 | async-start | bytes 1327104 | tf_op jit(solution)/shard_map/all_gather | solution.py:94
  10.0 147.1 %all-gather.16.cloned.1.call-start = ((), (), s32[]{:S(2)}) async-start(), calls=%async_computation.11 | async-start | bytes 5308416 | tf_op jit(solution)/shard_map/all_gather | solution.py:95
  10.6 198.6 %all-gather.18.cloned.1.call-start = ((), (), s32[]{:S(2)}) async-start(), calls=%async_computation.12 | async-start | bytes 5308416 | tf_op jit(solution)/shard_map/all_gather | solution.py:96
  11.2 222.7 %all-gather.20.cloned.1.call-start = ((), (), s32[]{:S(2)}) async-start(), calls=%async_computation.13 | async-start | bytes 1327104 | tf_op jit(solution)/shard_map/all_gather | solution.py:97
  11.9 314.9 %reduce-scatter.14.cloned.1.call-start = ((), (), s32[]{:S(2)}) async-start(), calls=%async_computation.17 | async-start | bytes 2654208 | tf_op jit(solution)/shard_map/reduce_scatter | solution.py:219
  54.0 12.9 %copy-start.27 = (f32[768]{0:T(1024)S(1)}, f32[768]{0:T(1024)}, u32[]{:S(2)}) copy-start(f32[768]{0:T(1024)} %param.26) | copy-start | bytes 9220
  71.7 14.4 %copy-start.8 = (bf16[512,768]{0,1:T(8,128)(2,1)}, bf16[512,768]{0,1:T(8,128)(2,1)S(1)}, u32[]{:S(2)}) copy-start(bf16[512,768]{0,1:T(8,128)(2,1)S(1)} %copy.52) | copy-start | bytes 2359300
  86.1 8.4 %copy-start.7 = (bf16[512,768]{0,1:T(8,128)(2,1)}, bf16[512,768]{0,1:T(8,128)(2,1)S(1)}, u32[]{:S(2)}) copy-start(bf16[512,768]{0,1:T(8,128)(2,1)S(1)} %copy.51) | copy-start | bytes 2359300
  105.7 51.5 %copy-start.25 = (f32[768]{0:T(1024)S(1)}, f32[768]{0:T(1024)}, u32[]{:S(2)}) copy-start(f32[768]{0:T(1024)} %param.27) | copy-start | bytes 9220
  108.1 56.4 %copy-start.5 = (f32[512,768]{1,0:T(8,128)}, f32[512,768]{1,0:T(8,128)S(1)}, u32[]{:S(2)}) copy-start(f32[512,768]{1,0:T(8,128)S(1)} %get-tuple-element.98) | copy-start | bytes 4718596
  164.5 53.2 %copy-start.30 = (f32[768]{0:T(1024)S(1)}, f32[768]{0:T(1024)}, u32[]{:S(2)}) copy-start(f32[768]{0:T(1024)} %param.28) | copy-start | bytes 9220
  217.7 18.3 %copy-start.28 = (f32[1,8,768]{2,1,0:T(8,128)S(1)}, f32[1,8,768]{2,1,0:T(8,128)}, u32[]{:S(2)}) copy-start(f32[1,8,768]{2,1,0:T(8,128)} %param.30) | copy-start | bytes 73732
  240.4 9.1 %slice-start = ((s8[4718592]{0:T(1024)(128)(4,1)}), s8[4194304]{0:T(1024)(128)(4,1)S(1)}, s32[]{:S(2)}) async-start(s8[4718592]{0:T(1024)(128)(4,1)} %bitcast.140), calls=%async_computation.22 | async-start | bytes 8388608
  240.8 12.1 %copy-start.14 = (f32[512,768]{1,0:T(8,128)}, f32[512,768]{1,0:T(8,128)S(1)}, u32[]{:S(2)}) copy-start(f32[512,768]{1,0:T(8,128)S(1)} %subtract_multiply_fusion) | copy-start | bytes 4718596
  240.8 8.7 %copy-start.6 = (f32[512,768]{1,0:T(8,128)S(1)}, f32[512,768]{1,0:T(8,128)}, u32[]{:S(2)}) copy-start(f32[512,768]{1,0:T(8,128)} %copy-done.5) | copy-start | bytes 4718596
  240.8 8.7 %slice-start.1 = ((s8[4718592]{0:T(1024)(128)(4,1)}), s8[524288]{0:T(1024)(128)(4,1)S(1)}, s32[]{:S(2)}) async-start(s8[4718592]{0:T(1024)(128)(4,1)} %bitcast.140), calls=%async_computation.23 | async-start | bytes 1048576
  256.3 72.2 %reduce-scatter.20.cloned.1.call-start = ((), (), s32[]{:S(2)}) async-start(), calls=%async_computation.20 | async-start | bytes 2654208 | tf_op jit(solution)/shard_map/reduce_scatter | solution.py:222
  259.8 104.8 %reduce-scatter.12.cloned.1.call-start = ((), (), s32[]{:S(2)}) async-start(), calls=%async_computation.16 | async-start | bytes 2654208 | tf_op jit(solution)/shard_map/reduce_scatter | solution.py:218
  275.5 127.0 %reduce-scatter.10.cloned.1.call-start = ((), (), s32[]{:S(2)}) async-start(), calls=%async_computation.15 | async-start | bytes 2654208 | tf_op jit(solution)/shard_map/reduce_scatter | solution.py:217
  296.0 144.3 %reduce-scatter.8.cloned.1.call-start = ((), (), s32[]{:S(2)}) async-start(), calls=%async_computation.14 | async-start | bytes 2654208 | tf_op jit(solution)/shard_map/reduce_scatter | solution.py:216
  303.3 238.8 %reduce-scatter.18.cloned.1.call-start = ((), (), s32[]{:S(2)}) async-start(), calls=%async_computation.19 | async-start | bytes 10616832 | tf_op jit(solution)/shard_map/reduce_scatter | solution.py:221
  313.7 328.6 %reduce-scatter.16.cloned.1.call-start = ((), (), s32[]{:S(2)}) async-start(), calls=%async_computation.18 | async-start | bytes 10616832 | tf_op jit(solution)/shard_map/reduce_scatter | solution.py:220
  322.5 411.1 %all-reduce.4.cloned.1.call-start = ((), (), s32[]{:S(2)}) async-start(), calls=%async_computation.21 | async-start | bytes 3833856 | tf_op jit(solution)/shard_map/psum | solution.py:225
  544.3 100.1 %copy-start.18 = (bf16[12,64,512]{2,1,0:T(8,128)(2,1)S(1)}, bf16[12,64,512]{2,1,0:T(8,128)(2,1)}, u32[]{:S(2)}) copy-start(bf16[12,64,512]{2,1,0:T(8,128)(2,1)} %copy-done.17) | copy-start | bytes 2359300
  663.3 11.6 %copy-start.11 = (bf16[12,64,512]{2,1,0:T(8,128)(2,1)S(1)}, bf16[12,64,512]{2,1,0:T(8,128)(2,1)}, u32[]{:S(2)}) copy-start(bf16[12,64,512]{2,1,0:T(8,128)(2,1)} %copy-done.10) | copy-start | bytes 2359300
  663.3 11.6 %copy-start.19 = (f32[512,768]{1,0:T(8,128)S(1)}, f32[512,768]{1,0:T(8,128)}, u32[]{:S(2)}) copy-start(f32[512,768]{1,0:T(8,128)} %fusion.82) | copy-start | bytes 4718596
  663.3 11.6 %copy-start.22 = (bf16[768,768]{1,0:T(8,128)(2,1)S(1)}, bf16[768,768]{1,0:T(8,128)(2,1)}, u32[]{:S(2)}) copy-start(bf16[768,768]{1,0:T(8,128)(2,1)} %all-gather.8.cloned.1.call-done) | copy-start | bytes 3538948
  679.4 7.7 %copy-start.33 = (f32[768]{0:T(1024)S(1)}, f32[768]{0:T(1024)}, u32[]{:S(2)}) copy-start(f32[768]{0:T(1024)} %get-tuple-element.65) | copy-start | bytes 9220
  679.4 51.2 %copy-start.31 = (f32[512]{0:T(512)S(1)}, f32[512]{0:T(512)}, u32[]{:S(2)}) copy-start(f32[512]{0:T(512)} %get-tuple-element.68) | copy-start | bytes 6148
  (21 other events, 82.5 us)
Sparse Core Ops, SparseCore 0:
  9.7 23.7 all-gather.11
  35.1 22.4 all-gather.9
  59.2 22.4 all-gather.7
  83.2 22.4 all-gather.13
  107.1 49.9 all-gather.15
  158.7 50.5 all-gather.17
  210.8 22.9 all-gather.19
  256.4 32.1 reduce-scatter.13
  290.9 35.7 reduce-scatter.19
  328.9 35.6 reduce-scatter.11
  366.9 35.5 reduce-scatter.9
  404.7 35.5 reduce-scatter.7
  442.6 99.5 reduce-scatter.17
  544.3 97.8 reduce-scatter.15
  647.2 69.2 all-reduce.3
where the time goes:
time: 761 us; the launch traced here: 750 us
  waiting for transfers between devices  434 us (57%)
  matrix products  140 us (18%)
  local copies, waits for them, and re-layouts  81.7 us (11%)
  blocking collectives  43.5 us (6%)
  other arithmetic  35.7 us (5%)
  between operations  14.9 us (2%)
    reduce_scatter x1, waiting for transfers between devices, per_device(): lax.psum_scatter(grad_down, 'fsdp', scatter_dimension=0, tiled=True)  100 us
    reduce_scatter x1, waiting for transfers between devices, per_device(): lax.psum_scatter(grad_up, 'fsdp', scatter_dimension=0, tiled=True)  97.9 us
    all_gather x1, waiting for transfers between devices, per_device(): lax.all_gather(w_up, 'fsdp', axis=0, tiled=True)  49 us
    unnamed x79, local copies, waits for them, and re-layouts  45 us
    all_gather x1, waiting for transfers between devices, per_device(): lax.all_gather(w_down, 'fsdp', axis=0, tiled=True)  44.7 us
    psum x1, blocking collectives, per_device(): lax.psum((grad_gain_attn, grad_gain_ffn, grad_gain_final, grad_table), ('...  43.5 us
    reduce_scatter x1, waiting for transfers between devices, per_device(): lax.psum_scatter(grad_key, 'fsdp', scatter_dimension=0, tiled=True)  36.3 us
    reduce_scatter x1, waiting for transfers between devices, per_device(): lax.psum_scatter(grad_query, 'fsdp', scatter_dimension=0, tiled=True)  36.1 us
  transfers between devices with their start and end apart: 15, of which 10 were waited for; matrix products, arithmetic and copies ran while one was open for 29% of the time, Pallas kernels for 0%

commit v1 on v0

--- a/solution.py
+++ b/solution.py
@@ -4,12 +4,15 @@
 import jax.numpy as jnp
 import numpy as np
 from jax import lax
+from jax.experimental import pallas as pl
+from jax.experimental.pallas import tpu as pltpu
 from jax.sharding import PartitionSpec as P
 
 REACH = 128
 
 
 EPSILON = 1e-06
+VMEM_BYTES = 60 * 2**20
 HIGH = lax.Precision.HIGHEST
 
 
@@ -65,7 +68,398 @@
     return jnp.where(same_doc, raw_scores + bias, -1e30)
 
 
+MESH = pl.DeviceIdType.MESH
+LANES = 128
+
+
+class Place:
+    def __init__(self):
+        self.dp, self.fsdp = lax.axis_index("dp"), lax.axis_index("fsdp")
+        self.y, self.x = self.dp // 2, self.dp % 2
+        self.z, self.c = self.fsdp // 2, self.fsdp % 2
+
+    def core(self):
+        return (self.dp, self.z * 2 + (1 - self.c))
+
+    def at_x(self):
+        return (self.y * 2 + (1 - self.x), self.fsdp)
+
+    def at_y(self):
+        return ((1 - self.y) * 2 + self.x, self.fsdp)
+
+    def at_xy(self):
+        return ((1 - self.y) * 2 + (1 - self.x), self.fsdp)
+
+    def up(self, d):
+        return lax.rem(self.z + d, 4)
+
+    def down(self, d):
+        return lax.rem(self.z + 4 - d, 4)
+
+    def at_z(self, d):
+        return (self.dp, self.up(d) * 2 + self.c)
+
+    def greet(self):
+        barrier = pltpu.get_barrier_semaphore()
+        partners = [self.core(), self.at_x(), self.at_y(), self.at_xy()]
+        partners += [self.at_z(d) for d in (1, 2, 3)]
+        for partner in partners:
+            pl.semaphore_signal(barrier, inc=1, device_id=partner, device_id_type=MESH)
+        pl.semaphore_wait(barrier, len(partners))
+
+
+def remote(src, dst, send, recv, device):
+    return pltpu.make_async_remote_copy(
+        src_ref=src, dst_ref=dst, send_sem=send, recv_sem=recv, device_id=device, device_id_type=MESH
+    )
+
+
+def half(which, size, start=0):
+    return pl.ds(pl.multiple_of(start + which * (size // 2), size // 2 if start % (size // 2) == 0 else 16), size // 2)
+
+
+class Unit:
+    def __init__(self, array, first, rows, left, wide):
+        self.array, self.first, self.rows, self.left, self.wide = array, first, rows, left, wide
+
+    def quarter(self, y, x):
+        return (half(y, self.rows, self.first), half(x, self.wide, self.left))
+
+    def whole(self):
+        return (pl.ds(self.first, self.rows), pl.ds(self.left, self.wide))
+
+
+class Gather:
+    RECVS = 13
+
+    def __init__(self, place, units, shards, wholes, send, recv):
+        self.p, self.units, self.shards, self.wholes = place, units, shards, wholes
+        self.send, self.recv = send, recv
+
+    def _part(self, u, z, y, x):
+        unit = self.units[u]
+        return self.wholes[unit.array].at[(z, self.p.c) + unit.quarter(y, x)]
+
+    def _z(self, u, d):
+        p, unit = self.p, self.units[u]
+        src = self.shards[unit.array].at[unit.quarter(p.y, p.x)]
+        return remote(src, self._part(u, p.z, p.y, p.x), self.send.at[u, d - 1], self.recv.at[u, d - 1], p.at_z(d))
+
+    def _hop(self, u, d, kind, y, x, device):
+        ref = self._part(u, self.p.down(d), y, x)
+        k = 3 * kind + d - 1
+        return remote(ref, ref, self.send.at[u, k], self.recv.at[u, k], device)
+
+    def _to_x(self, u, d):
+        return self._hop(u, d, 1, self.p.y, self.p.x, self.p.at_x())
+
+    def _to_y(self, u, d):
+        return self._hop(u, d, 2, self.p.y, self.p.x, self.p.at_y())
+
+    def _through_x(self, u, d):
+        return (u + d) % 2 == 0
+
+    def _diagonal(self, u, d):
+        p = self.p
+        if self._through_x(u, d):
+            return self._hop(u, d, 3, p.y, 1 - p.x, p.at_y())
+        return self._hop(u, d, 3, 1 - p.y, p.x, p.at_x())
+
+    def _core(self, u):
+        unit = self.units[u]
+        ref = self.wholes[unit.array].at[(slice(None), self.p.c) + unit.whole()]
+        return remote(ref, ref, self.send.at[u, 12], self.recv.at[u, 12], self.p.core())
+
+    def start(self, u):
+        for d in (1, 2, 3):
+            self._z(u, d).start()
+
+    def plane(self, u):
+        for d in (1, 2, 3):
+            self._z(u, d).wait_recv()
+            self._to_x(u, d).start()
+            self._to_y(u, d).start()
+
+    def corner(self, u):
+        for d in (1, 2, 3):
+            first, second = (self._to_x, self._to_y) if self._through_x(u, d) else (self._to_y, self._to_x)
+            first(u, d).wait_recv()
+            self._diagonal(u, d).start()
+            second(u, d).wait_recv()
+
+    def pair(self, u):
+        for d in (1, 2, 3):
+            self._diagonal(u, d).wait_recv()
+        self._core(u).start()
+
+    def arrive(self, u):
+        self._core(u).wait_recv()
+
+    def finish(self, u):
+        for d in (1, 2, 3):
+            self._z(u, d).wait_send()
+            self._to_x(u, d).wait_send()
+            self._to_y(u, d).wait_send()
+            self._diagonal(u, d).wait_send()
+        self._core(u).wait_send()
+
+
+def gather_units():
+    small = [Unit(i, 0, 96, 0, 768) for i in range(4)]
+    up = [Unit(4, 0, 96, 768 * j, 768) for j in range(4)]
+    down = [Unit(5, 128 * j, 128, 0, 768) for j in range(3)]
+    return small + up + [Unit(6, 0, 96, 0, 768)] + down
+
+
+def gather_kernel(units, *refs):
+    shards, outs, wholes = refs[:7], refs[7:14], refs[14:21]
+    send, recv, local = refs[21:]
+    place = Place()
+    gather = Gather(place, units, shards, wholes, send, recv)
+    own = [
+        pltpu.make_async_copy(shard, whole.at[place.z, place.c], local.at[i])
+        for i, (shard, whole) in enumerate(zip(shards, wholes))
+    ]
+    for copy in own:
+        copy.start()
+    place.greet()
+    for u in range(len(units)):
+        gather.start(u)
+    for copy in own:
+        copy.wait()
+    stages = (gather.plane, gather.corner, gather.pair, gather.arrive)
+    for step in range(len(units) + len(stages) - 1):
+        for lag, stage in enumerate(stages):
+            if 0 <= step - lag < len(units):
+                stage(step - lag)
+    back = [
+        pltpu.make_async_copy(whole, out, local.at[i])
+        for i, (whole, out) in enumerate(zip(wholes, outs))
+    ]
+    for copy in back:
+        copy.start()
+    for u in range(len(units)):
+        gather.finish(u)
+    for copy in back:
+        copy.wait()
+
+
+def gather_all(shards):
+    units = gather_units()
+    full = [(4, 2) + shard.shape for shard in shards]
+    wholes = pl.pallas_call(
+        partial(gather_kernel, units),
+        out_shape=[jax.ShapeDtypeStruct(shape, jnp.bfloat16) for shape in full],
+        in_specs=[pl.BlockSpec(memory_space=pl.ANY)] * 7,
+        out_specs=[pl.BlockSpec(memory_space=pl.ANY)] * 7,
+        scratch_shapes=[pltpu.VMEM(shape, jnp.bfloat16) for shape in full]
+        + [
+            pltpu.SemaphoreType.DMA((len(units), Gather.RECVS)),
+            pltpu.SemaphoreType.DMA((len(units), Gather.RECVS)),
+            pltpu.SemaphoreType.DMA((7,)),
+        ],
+        compiler_params=pltpu.CompilerParams(
+            collective_id=0, has_side_effects=True, vmem_limit_bytes=VMEM_BYTES
+        ),
+        name="gather_weights",
+    )(*shards)
+    return [whole.reshape(-1, whole.shape[-1]) for whole in wholes]
+
+
+class Reduce:
+    SEMS = 12
+
+    def __init__(self, place, grad, core, along_x, along_y, second_x, second_y, line, total, send, recv):
+        self.p, self.g, self.rc = place, grad, core
+        self.rx, self.ry, self.sx, self.sy, self.rz, self.f = along_x, along_y, second_x, second_y, line, total
+        self.send, self.recv = send, recv
+        self.rows = grad.shape[2]
+        rows = self.rows
+        p = place
+        self.row = [half(i, rows) for i in (p.y, 1 - p.y)]
+        self.col = [half(i, 768) for i in (p.x, 1 - p.x)]
+
+    def _copy(self, k, src, dst, device):
+        return remote(src, dst, self.send.at[k], self.recv.at[k], device)
+
+    def _core(self):
+        return self._copy(0, self.g.at[:, 1 - self.p.c], self.rc, self.p.core())
+
+    def _first(self):
+        p, low, high = self.p, pl.ds(0, 2), pl.ds(2, 2)
+        return (
+            self._copy(1, self.g.at[low, p.c, :, self.col[1]], self.rx, p.at_x()),
+            self._copy(2, self.g.at[high, p.c, self.row[1], :], self.ry, p.at_y()),
+        )
+
+    def _second(self):
+        p, low, high = self.p, pl.ds(0, 2), pl.ds(2, 2)
+        return (
+            self._copy(3, self.g.at[low, p.c, self.row[1], self.col[0]], self.sy, p.at_y()),
+            self._copy(4, self.g.at[high, p.c, self.row[0], self.col[1]], self.sx, p.at_x()),
+        )
+
+    def _line(self):
+        p = self.p
+        return [
+            self._copy(4 + d, self.g.at[p.up(d), p.c, self.row[0], self.col[0]], self.rz.at[d - 1], p.at_z(d))
+            for d in (1, 2, 3)
+        ]
+
+    def _spread(self):
+        p, part = self.p, self.f.at[self.row[0], self.col[0]]
+        return [self._copy(8 + i, part, part, device) for i, device in enumerate((p.at_x(), p.at_y(), p.at_xy()))]
+
+    def _add(self, ref, other):
+        ref[...] = (ref[...].astype(jnp.float32) + other[...].astype(jnp.float32)).astype(jnp.bfloat16)
+
+    def start(self):
+        self._core().start()
+
+    def first(self):
+        p = self.p
+        self._core().wait_recv()
+        for i in range(4):
+            self._add(self.g.at[i, p.c], self.rc.at[i])
+        for copy in self._first():
+            copy.start()
+
+    def second(self):
+        p = self.p
+        along_x, along_y = self._first()
+        along_x.wait_recv()
+        for i in range(2):
+            self._add(self.g.at[i, p.c, :, self.col[0]], self.rx.at[i])
+        to_y, to_x = self._second()
+        to_y.start()
+        along_y.wait_recv()
+        for i in range(2):
+            self._add(self.g.at[2 + i, p.c, self.row[0], :], self.ry.at[i])
+        to_x.start()
+
+    def line(self):
+        p = self.p
+        for copy in self._second():
+            copy.wait_recv()
+        for i in range(2):
+            self._add(self.g.at[i, p.c, self.row[0], self.col[0]], self.sy.at[i])
+            self._add(self.g.at[2 + i, p.c, self.row[0], self.col[0]], self.sx.at[i])
+        for copy in self._line():
+            copy.start()
+
+    def spread(self):
+        p = self.p
+        total = self.g[p.z, p.c, self.row[0], self.col[0]].astype(jnp.float32)
+        for d, copy in enumerate(self._line()):
+            copy.wait_recv()
+            total = total + self.rz[d].astype(jnp.float32)
+        self.f[self.row[0], self.col[0]] = total.astype(jnp.bfloat16)
+        for copy in self._spread():
+            copy.start()
+
+    def arrive(self):
+        for copy in self._spread():
+            copy.wait_recv()
+
+    def finish(self):
+        for copy in (self._core(), *self._first(), *self._second(), *self._line(), *self._spread()):
+            copy.wait_send()
+
+
+def reduce_scratch(rows):
+    shapes = [
+        (4, rows, 768),
+        (2, rows, 384),
+        (2, rows // 2, 768),
+        (2, rows // 2, 384),
+        (2, rows // 2, 384),
+        (3, rows // 2, 384),
+        (rows, 768),
+    ]
+    return shapes
+
+
+def reduce_kernel(counts, *refs):
+    small, tall = counts
+    grads, outs, refs = refs[:7], refs[7:14], refs[14:]
+    held, refs = refs[:2], refs[2:]
+    buffers, refs = (refs[:7], refs[7:14]), refs[14:]
+    send, recv, local = refs
+    place = Place()
+    order = [(0, 0, 6, 0)]
+    order += [(1, j, 5, j) for j in range(tall)]
+    order += [(0, 1 + j, 4, j) for j in range(4)]
+    order += [(0, 5, 3, 0), (0, 6, 2, 0), (0, 7, 0, 0), (0, 8, 1, 0)]
+    loads, works, writes = [], [], []
+    for u, (kind, slot, array, j) in enumerate(order):
+        hold = held[kind].at[slot]
+        if array == 5:
+            src = grads[5].at[:, :, pl.ds(128 * j, 128), :]
+            dst = outs[5].at[pl.ds(128 * j, 128), :]
+        else:
+            src = grads[array].at[:, :, :, pl.ds(768 * j, 768)]
+            dst = outs[array].at[:, pl.ds(768 * j, 768)]
+        loads.append(pltpu.make_async_copy(src, hold, local.at[u, 0]))
+        parts = [b.at[slot] for b in buffers[kind]]
+        works.append(Reduce(place, hold, *parts, send.at[u], recv.at[u]))
+        writes.append(pltpu.make_async_copy(parts[-1], dst, local.at[u, 1]))
+    for copy in loads:
+        copy.start()
+    place.greet()
+    n = len(order)
+
+    def begin(u):
+        loads[u].wait()
+        works[u].start()
+
+    def end(u):
+        works[u].arrive()
+        writes[u].start()
+
+    stages = (
+        begin,
+        lambda u: works[u].first(),
+        lambda u: works[u].second(),
+        lambda u: works[u].line(),
+        lambda u: works[u].spread(),
+        end,
+    )
+    for step in range(n + len(stages) - 1):
+        for lag, stage in enumerate(stages):
+            if 0 <= step - lag < n:
+                stage(step - lag)
+    for u in range(n):
+        works[u].finish()
+        writes[u].wait()
+
+
+def reduce_all(grads):
+    grads = [g.astype(jnp.bfloat16).reshape(4, 2, g.shape[0] // 8, g.shape[1]) for g in grads]
+    small, tall = 9, 3
+    scratch = [pltpu.VMEM((small, 4, 2, 96, 768), jnp.bfloat16), pltpu.VMEM((tall, 4, 2, 128, 768), jnp.bfloat16)]
+    for count, rows in ((small, 96), (tall, 128)):
+        scratch += [pltpu.VMEM((count,) + shape, jnp.bfloat16) for shape in reduce_scratch(rows)]
+    n = small + tall
+    return pl.pallas_call(
+        partial(reduce_kernel, (small, tall)),
+        out_shape=[jax.ShapeDtypeStruct(g.shape[2:], jnp.bfloat16) for g in grads],
+        in_specs=[pl.BlockSpec(memory_space=pl.ANY)] * 7,
+        out_specs=[pl.BlockSpec(memory_space=pl.ANY)] * 7,
+        scratch_shapes=scratch
+        + [
+            pltpu.SemaphoreType.DMA((n, Reduce.SEMS)),
+            pltpu.SemaphoreType.DMA((n, Reduce.SEMS)),
+            pltpu.SemaphoreType.DMA((n, 2)),
+        ],
+        compiler_params=pltpu.CompilerParams(
+            collective_id=1, has_side_effects=True, vmem_limit_bytes=VMEM_BYTES
+        ),
+        name="reduce_gradients",
+    )(*grads)
+
+
 def per_device(
+    near,
     inputs,
     seg_ids,
     pool_index,
@@ -87,15 +481,8 @@
     head_dim = width // heads
     tokens = rows * length
     head_shape = (rows, length, heads, head_dim)
-    gathered = (
-        lax.all_gather(w_query, "fsdp", axis=0, tiled=True),
-        lax.all_gather(w_key, "fsdp", axis=0, tiled=True),
-        lax.all_gather(w_value, "fsdp", axis=0, tiled=True),
-        lax.all_gather(w_out, "fsdp", axis=0, tiled=True),
-        lax.all_gather(w_up, "fsdp", axis=0, tiled=True),
-        lax.all_gather(w_down, "fsdp", axis=0, tiled=True),
-        lax.all_gather(w_proj, "fsdp", axis=0, tiled=True),
-    )
+    shards = (w_query, w_key, w_value, w_out, w_up, w_down, w_proj)
+    gathered = gather_all(shards) if near else [lax.all_gather(w, "fsdp", axis=0, tiled=True) for w in shards]
     full_query, full_key, full_value, full_out, full_up, full_down, full_proj = gathered
     flat = inputs.reshape(tokens, width).astype(jnp.float32)
     normed_one, factor_one = rms_forward(flat, gain_attn)
@@ -147,16 +534,7 @@
         tokens, width
     )
     stream_two, grad_gain_final = rms_backward(hidden_two, factor_three, gain_final, final_grad)
-    back_weights = (
-        lax.all_gather(w_query, "fsdp", axis=0, tiled=True),
-        lax.all_gather(w_key, "fsdp", axis=0, tiled=True),
-        lax.all_gather(w_value, "fsdp", axis=0, tiled=True),
-        lax.all_gather(w_out, "fsdp", axis=0, tiled=True),
-        lax.all_gather(w_up, "fsdp", axis=0, tiled=True),
-        lax.all_gather(w_down, "fsdp", axis=0, tiled=True),
-        lax.all_gather(w_proj, "fsdp", axis=0, tiled=True),
-    )
-    back_query, back_key, back_value, back_out, back_up, back_down, back_proj = back_weights
+    back_query, back_key, back_value, back_out, back_up, back_down, back_proj = gathered
     ffn_grad = stream_two.astype(jnp.bfloat16)
     grad_down = matmul_left(activated, ffn_grad)
     act_grad = matmul_right(ffn_grad, back_down)
@@ -212,24 +590,12 @@
     )
     stream_in, grad_gain_attn = rms_backward(flat, factor_one, gain_attn, normed_one_grad)
     input_grad = (stream_one + stream_in).reshape(rows, length, width)
-    shard_query, shard_key, shard_value, shard_out, shard_up, shard_down, shard_proj = (
-        lax.psum_scatter(grad_query, "fsdp", scatter_dimension=0, tiled=True),
-        lax.psum_scatter(grad_key, "fsdp", scatter_dimension=0, tiled=True),
-        lax.psum_scatter(grad_value, "fsdp", scatter_dimension=0, tiled=True),
-        lax.psum_scatter(grad_out, "fsdp", scatter_dimension=0, tiled=True),
-        lax.psum_scatter(grad_up, "fsdp", scatter_dimension=0, tiled=True),
-        lax.psum_scatter(grad_down, "fsdp", scatter_dimension=0, tiled=True),
-        lax.psum_scatter(grad_proj, "fsdp", scatter_dimension=0, tiled=True),
-    )
-    summed = (
-        lax.psum(shard_query.astype(jnp.bfloat16), "dp").astype(jnp.float32),
-        lax.psum(shard_key.astype(jnp.bfloat16), "dp").astype(jnp.float32),
-        lax.psum(shard_value.astype(jnp.bfloat16), "dp").astype(jnp.float32),
-        lax.psum(shard_out.astype(jnp.bfloat16), "dp").astype(jnp.float32),
-        lax.psum(shard_up.astype(jnp.bfloat16), "dp").astype(jnp.float32),
-        lax.psum(shard_down.astype(jnp.bfloat16), "dp").astype(jnp.float32),
-        lax.psum(shard_proj.astype(jnp.bfloat16), "dp").astype(jnp.float32),
-    )
+    grads = (grad_query, grad_key, grad_value, grad_out, grad_up, grad_down, grad_proj)
+    if near:
+        summed = [shard.astype(jnp.float32) for shard in reduce_all(grads)]
+    else:
+        shards = [lax.psum_scatter(g, "fsdp", scatter_dimension=0, tiled=True) for g in grads]
+        summed = [lax.psum(shard.astype(jnp.bfloat16), "dp").astype(jnp.float32) for shard in shards]
     smalls = lax.psum((grad_gain_attn, grad_gain_ffn, grad_gain_final, grad_table), ("dp", "fsdp"))
     return (
         embeddings,
@@ -249,8 +615,9 @@
 
 
 def solution(mesh):
+    near = (mesh.shape["dp"], mesh.shape["fsdp"]) == (4, 8)
     return jax.shard_map(
-        per_device,
+        partial(per_device, near),
         mesh=mesh,
         in_specs=(
             P(("dp", "fsdp"), None, None),

time: 761 us -> 433 us (0.57)
  waiting for transfers between devices: 434 us -> 0 us
  Pallas kernels: 0 us -> 168 us
  matrix products: 140 us -> 108 us
  between operations: 14.9 us -> 1.61 us
  other arithmetic: 35.7 us -> 24.9 us
    reduce_scatter x7 -> x0, waiting for transfers between devices: 305 us -> none  [the longest x1 100 us: per_device(): lax.psum_scatter(grad_down, 'fsdp', scatter_dimension=0, tiled=True)]
    pallas_call x0 -> x2, Pallas kernels: none -> 168 us  [the longest x1 96.3 us: reduce_all(): pl.pallas_call(partial(reduce_kernel, (small, tall)), out_shape=[jax.Shap...]
    all_gather x7 -> x0, waiting for transfers between devices: 125 us -> none  [the longest x1 49 us: per_device(): lax.all_gather(w_up, 'fsdp', axis=0, tiled=True)]
    convert_element_type x14 -> x7, other arithmetic: 22.1 us -> 9.64 us  [per_device(): summed = [shard.astype(jnp.float32) for shard in reduce_all(grads)]]
    dot_general x7, matrix products: 33.6 us -> 22.7 us  [matmul_right(): lax.dot_general(left, right, (((1,), (1,)), ((), ())), preferred_element_...]
    dot_general x6, matrix products: 28.5 us -> 18.6 us  [matmul_left(): lax.dot_general(left, right, (((0,), (0,)), ((), ())), preferred_element_...]
    dot_general x6, matrix products: 25.6 us -> 17.7 us  [matmul(): return jnp.dot(left, right, preferred_element_type=jnp.float32)]
    unnamed x79 -> x77, local copies, waits for them, and re-layouts: 45 us -> 44.4 us
  transfers between devices with their start and end apart: 15 -> 0, of which waited for: 10 -> 0; matrix products, arithmetic and copies ran while one was open for 29% -> 0% of each run, Pallas kernels for 0% -> 0%
where the time goes in v1:
time: 433 us; the launch traced here: 428 us
  Pallas kernels  168 us (39%)
  matrix products  108 us (25%)
  local copies, waits for them, and re-layouts  83.1 us (19%)
  blocking collectives  42.3 us (10%)
  other arithmetic  24.9 us (6%)
    pallas_call x1, Pallas kernels, reduce_all(): pl.pallas_call(partial(reduce_kernel, (small, tall)), out_shape=[jax.Shap...  96.3 us
    pallas_call x1, Pallas kernels, gather_all(): pl.pallas_call(partial(gather_kernel, units), out_shape=[jax.ShapeDtypeSt...  71.5 us
    unnamed x77, local copies, waits for them, and re-layouts  44.4 us
    psum x1, blocking collectives, per_device(): lax.psum((grad_gain_attn, grad_gain_ffn, grad_gain_final, grad_table), ('...  42.3 us
    reshape x2, local copies, waits for them, and re-layouts, per_device(): jnp.dot(bias_table.T, onehot_cols.astype(jnp.float32), precision=HIGH)  23.2 us
    dot_general x7, matrix products, matmul_right(): lax.dot_general(left, right, (((1,), (1,)), ((), ())), preferred_element_...  22.7 us
    dot_general x6, matrix products, matmul_left(): lax.dot_general(left, right, (((0,), (0,)), ((), ())), preferred_element_...  18.6 us
    dot_general x6, matrix products, matmul(): return jnp.dot(left, right, preferred_element_type=jnp.float32)  17.7 us

profile of v1, /device:TPU:12, one launch (start us, length us, event | category | flops | bytes accessed | tf_op | source)
XLA Modules:
  0.0 427.9 jit_solution(7656548287896743136)
XLA Ops:
  4.0 71.5 %gather_weights.1 = (bf16[4,2,96,768]{3,2,1,0:T(8,128)(2,1)}, bf16[4,2,96,768]{3,2,1,0:T(8,128)(2,1)}, bf16[4,2,96,768]{3,2,1,0:T(8,128)(2,1)}, bf16[4,2,96,768]...) custom-call(bf16[96,768]{1,0:T(8,128)(2,1)} %refs_0_.1, ...), custom_call_target="tpu_custom_call" | custom-call | tf_op jit(solution)/shard_map/gather_weights/pallas_call | solution.py:250
  75.5 3.0 convolution_convert_fusion.9
  83.2 3.0 convolution_convert_fusion.8
  87.6 12.2 %fusion.1 = f32[262144,12]{0,1:T(8,128)S(1)} fusion(f32[32,12]{0,1:T(8,128)S(1)} %copy-done, s32[262144]{0:T(1024)} %constant.78), kind=kOutput, calls=%fused_computation.2 | convolution fusion | flops 1216348160 | bytes 13633024 | tf_op jit(solution)/shard_map/dot_general | solution.py:497
  99.9 19.1 %copy.65 = f32[2,8,512,512]{3,2,1,0:T(8,128)} copy(f32[2,8,512,512]{3,1,2,0:T(8,128)S(1)} %bitcast.136) | data formatting | bytes 33554432
  119.0 10.6 %slice = f32[12,512,512]{2,1,0:T(8,128)} slice(f32[16,512,512]{2,1,0:T(8,128)} %bitcast.137), slice={[0:12], [0:512], [0:512]} | slice | bytes 25165824 | tf_op jit(solution)/shard_map/reshape | solution.py:497
  129.6 12.6 %copy.54 = f32[12,512,512]{1,2,0:T(8,128)} copy(f32[12,512,512]{2,1,0:T(8,128)} %slice) | data formatting | bytes 25165824 | tf_op jit(solution)/shard_map/reshape | solution.py:497
  142.2 6.6 %fusion.72 = (f32[12,512]{1,0:T(8,128)S(1)}, f32[12,512,512]{1,2,0:T(8,128)S(1)}) fusion(f32[12,512,512]{1,2,0:T(8,128)} %copy.54, bf16[512,12,64]{0,2,1:T(8,128)(2,1)S(1)} %bitcast.146, bf16[512,12,64]{0,2,1:T(8,128)(2,1)S(1)} %bitcast.139, pred[512,512]{0,1:T(8,128)(4,1)S(1)} %broadcast_compare_fusion), kind=kOutput, calls=%fused_computation.104 | convolution fusion | flops 412084224 | bytes 27025408 | tf_op jit(solution)/shard_map/while/body/eval_jaxpr/qhd,khd->hqk/dot_general | solution.py:66
  150.7 2.6 copy-done.2
  153.3 2.1 fusion.33
  156.4 5.2 %fusion.65 = f32[512,3072]{1,0:T(8,128)S(1)} fusion(bf16[768,3072]{1,0:T(8,128)(2,1)} %bitcast.148, f32[512,768]{1,0:T(8,128)S(1)} %get-tuple-element.119, f32[768]{0:T(1024)S(1)} %copy-done.21, f32[512]{0:T(512)S(1)} %add_rsqrt_fusion.1), kind=kOutput, calls=%fused_computation.103 | convolution fusion | flops 2417098752 | bytes 12588032 | tf_op jit(solution)/shard_map/dot_general | solution.py:50
  161.6 3.9 multiply_reduce_fusion.5
  169.3 3.1 convolution_convert_fusion.6
  174.1 6.3 %fusion.11 = bf16[512,3072]{1,0:T(8,128)(2,1)S(1)} fusion(f32[512,3072]{1,0:T(8,128)S(1)} %fusion.65, bf16[3072,768]{1,0:T(8,128)(2,1)S(1)} %bitcast.181, f32[512,768]{1,0:T(8,128)S(1)} %subtract_multiply_fusion), kind=kOutput, calls=%fused_computation.19 | convolution fusion | flops 2447769600 | bytes 15728640 | tf_op jit(solution)/shard_map/dot_general | solution.py:60
  180.4 2.9 multiply_reduce_fusion.2
  183.3 5.1 %convolution_convert_fusion = bf16[3072,768]{1,0:T(8,128)(2,1)} fusion(f32[512,768]{1,0:T(8,128)S(1)} %subtract_multiply_fusion, f32[512,3072]{1,0:T(8,128)S(1)} %fusion.65), kind=kOutput, calls=%fused_computation.21 | convolution fusion | flops 2432827392 | bytes 12582912 | tf_op jit(solution)/shard_map/dot_general | solution.py:54
  191.4 4.5 %convolution_convert_fusion.1 = bf16[768,3072]{1,0:T(8,128)(2,1)} fusion(bf16[512,3072]{1,0:T(8,128)(2,1)S(1)} %fusion.11, f32[512,768]{1,0:T(8,128)S(1)} %get-tuple-element.119, f32[768]{0:T(1024)S(1)} %copy-done.21, f32[512]{0:T(512)S(1)} %add_rsqrt_fusion.1), kind=kOutput, calls=%fused_computation.22 | convolution fusion | flops 2419458048 | bytes 9442304 | tf_op jit(solution)/shard_map/dot_general | solution.py:54
  195.9 2.3 copy.56
  198.2 3.0 convolution_convert_fusion.2
  201.2 6.7 %fusion.36 = bf16[12,64,512]{2,1,0:T(8,128)(2,1)S(1)} fusion(bf16[512,12,64]{0,2,1:T(8,128)(2,1)S(1)} %bitcast.144, f32[12,512,512]{1,2,0:T(8,128)} %copy-done.2, f32[12,512]{1,0:T(8,128)S(1)} %log_add_fusion), kind=kOutput, calls=%fused_computation.65 | convolution fusion | flops 409337856 | bytes 14180352 | tf_op jit(solution)/shard_map/while/body/eval_jaxpr/hqk,qhd->khd/dot_general | solution.py:567
  207.9 2.0 convolution_convert_fusion.3
  210.0 10.5 %multiply_reduce_fusion = (f32[12,512]{1,0:T(8,128)S(1)}, f32[12,512,512]{1,2,0:T(8,128)}) fusion(f32[12,512,512]{1,2,0:T(8,128)} %copy-done.2, f32[12,512]{1,0:T(8,128)S(1)} %log_add_fusion, bf16[512,12,64]{0,2,1:T(8,128)(2,1)S(1)} %bitcast.145, bf16[512,12,64]{0,2,1:T(8,128)(2,1)S(1)} %bitcast.143), kind=kOutput, calls=%fused_computation.6 | convolution fusion | flops 412084224 | bytes 26787840 | tf_op jit(solution)/shard_map/while/body/eval_jaxpr/qhd,khd->hqk/dot_general | solution.py:555
  222.6 7.0 %multiply_convert_fusion = bf16[12,512,512]{1,2,0:T(8,128)(2,1)S(1)} fusion(f32[12,512,512]{1,2,0:T(8,128)} %get-tuple-element.127, f32[12,512,512]{1,2,0:T(8,128)S(1)} %bitcast.135, f32[12,512]{1,0:T(8,128)S(1)} %get-tuple-element.126, f32[12,512]{1,0:T(8,128)S(1)} %log_add_fusion), kind=kLoop, calls=%fused_computation.5 | loop fusion | flops 12582912 | bytes 31506432 | tf_op jit(solution)/shard_map/while/body/eval_jaxpr/convert_element_type | solution.py:560
  229.6 2.9 convolution_convert_fusion.11
  233.7 8.8 %copy.60 = bf16[12,512,512]{2,1,0:T(8,128)(2,1)} copy(bf16[12,512,512]{1,2,0:T(8,128)(2,1)} %copy-done.3) | data formatting | bytes 12582912 | tf_op jit(solution)/shard_map/while/body/eval_jaxpr/convert_element_type | solution.py:560
  242.5 2.2 fusion.73
  244.7 2.0 convolution_convert_fusion.5
  253.0 96.3 %reduce_gradients.1 = (bf16[96,768]{1,0:T(8,128)(2,1)}, bf16[96,768]{1,0:T(8,128)(2,1)}, bf16[96,768]{1,0:T(8,128)(2,1)}, bf16[96,768]{1,0:T(8,128)(2,1)}, bf16[...) custom-call(bf16[4,2,96,768]{3,2,1,0:T(8,128)(2,1)} %bitcast.167, ...), custom_call_target="tpu_custom_call" | custom-call | tf_op jit(solution)/shard_map/reduce_gradients/pallas_call | solution.py:443
  359.1 7.0 %pad = bf16[16,512,512]{2,1,0:T(8,128)(2,1)} pad(bf16[12,512,512]{2,1,0:T(8,128)(2,1)} %copy.60, bf16[]{:T(256)} %constant.79), padding=0_4x0_0x0_0 | pad | bytes 14680066
  366.0 11.5 %copy.66 = bf16[2,8,512,512]{3,1,2,0:T(8,128)(2,1)} copy(bf16[2,8,512,512]{3,2,1,0:T(8,128)(2,1)} %bitcast.138) | data formatting | bytes 16777216
  377.5 7.6 %fusion = f32[32,12]{0,1:T(8,128)S(1)} fusion(bf16[12,262144]{1,0:T(8,128)(2,1)} %bitcast.141, s32[262144]{0:T(1024)S(1)} %copy-done.13), kind=kOutput, calls=%fused_computation.1 | convolution fusion | flops 209715200 | bytes 7341568 | tf_op jit(solution)/shard_map/while/body/eval_jaxpr/dot_general | solution.py:60
  385.1 42.3 %all-reduce = (f32[768]{0:T(1024)}, f32[768]{0:T(1024)}, f32[768]{0:T(1024)}, f32[32,12]{0,1:T(8,128)}) all-reduce(f32[768]{0:T(1024)S(1)} %get-tuple-element.108, f32[768]{0:T(1024)S(1)} %get-tuple-element.106, f32[768]{0:T(1024)S(1)} %get-tuple-element.104, f32[32,12]{0,1:T(8,128)S(1)} %fusion), channel_id=1, replica_groups=mesh['dp'=4,'fsdp'=8] {'dp','fsdp'}, use_global_device_ids=true, to_apply=%region_13.14 | all-reduce | flops 2688 | bytes 21504 | tf_op jit(solution)/shard_map/psum | solution.py:599
  (113 shorter events, 39.8 us)
Async XLA Ops:
  0.6 87.0 %copy-start = (f32[32,12]{0,1:T(8,128)S(1)}, f32[32,12]{0,1:T(8,128)}, u32[]{:S(2)}) copy-start(f32[32,12]{0,1:T(8,128)} %param.29) | copy-start | bytes 4612
  0.7 74.8 %copy-start.7 = (bf16[1,512,768]{2,1,0:T(8,128)(2,1)S(1)}, bf16[1,512,768]{2,1,0:T(8,128)(2,1)}, u32[]{:S(2)}) copy-start(bf16[1,512,768]{2,1,0:T(8,128)(2,1)} %param.16) | copy-start | bytes 2359300
  0.7 74.8 %copy-start.25 = (f32[768]{0:T(1024)S(1)}, f32[768]{0:T(1024)}, u32[]{:S(2)}) copy-start(f32[768]{0:T(1024)} %param.26) | copy-start | bytes 9220
  78.5 1.5 copy-start.15
  80.0 62.1 %copy-start.5 = (bf16[512,768]{0,1:T(8,128)(2,1)}, bf16[512,768]{0,1:T(8,128)(2,1)S(1)}, u32[]{:S(2)}) copy-start(bf16[512,768]{0,1:T(8,128)(2,1)S(1)} %copy.52) | copy-start | bytes 2359300
  148.8 4.5 %copy-start.2 = (f32[12,512,512]{1,2,0:T(8,128)}, f32[12,512,512]{1,2,0:T(8,128)S(1)}, u32[]{:S(2)}) copy-start(f32[12,512,512]{1,2,0:T(8,128)S(1)} %get-tuple-element.117) | copy-start | bytes 37748740
  153.3 2.1 copy-start.28
  155.4 6.2 %slice-start.5 = ((s8[4718592]{0:T(1024)(128)(4,1)}), s8[4194304]{0:T(1024)(128)(4,1)S(1)}, s32[]{:S(2)}) async-start(s8[4718592]{0:T(1024)(128)(4,1)} %bitcast.178), calls=%async_computation.5 | async-start | bytes 8388608
  156.4 5.2 %slice-start.6 = ((s8[4718592]{0:T(1024)(128)(4,1)}), s8[524288]{0:T(1024)(128)(4,1)S(1)}, s32[]{:S(2)}) async-start(s8[4718592]{0:T(1024)(128)(4,1)} %bitcast.178), calls=%async_computation.6 | async-start | bytes 1048576
  161.6 3.9 copy-start.23
  161.6 3.9 copy-start.24
  161.6 3.9 copy-start.26
  165.5 2.0 copy-start.22
  173.7 6.7 %slice-start.3 = ((s8[4718592]{0:T(1024)(128)(4,1)}), s8[4194304]{0:T(1024)(128)(4,1)S(1)}, s32[]{:S(2)}) async-start(s8[4718592]{0:T(1024)(128)(4,1)} %bitcast.149), calls=%async_computation.3 | async-start | bytes 8388608
  174.1 6.4 %slice-start.4 = ((s8[4718592]{0:T(1024)(128)(4,1)}), s8[524288]{0:T(1024)(128)(4,1)S(1)}, s32[]{:S(2)}) async-start(s8[4718592]{0:T(1024)(128)(4,1)} %bitcast.149), calls=%async_computation.4 | async-start | bytes 1048576
  198.2 3.0 copy-start.4
  201.2 6.7 %copy-start.8 = (bf16[1,512,768]{2,1,0:T(8,128)(2,1)S(1)}, bf16[1,512,768]{2,1,0:T(8,128)(2,1)}, u32[]{:S(2)}) copy-start(bf16[1,512,768]{2,1,0:T(8,128)(2,1)} %param.16) | copy-start | bytes 2359300
  207.9 2.0 copy-start.11
  210.0 10.5 %slice-start = ((s8[12582912]{0:T(1024)(128)(4,1)}), s8[4194304]{0:T(1024)(128)(4,1)S(1)}, s32[]{:S(2)}) async-start(s8[12582912]{0:T(1024)(128)(4,1)} %bitcast.134), calls=%async_computation | async-start | bytes 8388608
  210.0 11.3 %slice-start.1 = ((s8[12582912]{0:T(1024)(128)(4,1)}), s8[4194304]{0:T(1024)(128)(4,1)S(1)}, s32[]{:S(2)}) async-start(s8[12582912]{0:T(1024)(128)(4,1)} %bitcast.134), calls=%async_computation.1 | async-start | bytes 8388608
  210.0 12.6 %slice-start.2 = ((s8[12582912]{0:T(1024)(128)(4,1)}), s8[4194304]{0:T(1024)(128)(4,1)S(1)}, s32[]{:S(2)}) async-start(s8[12582912]{0:T(1024)(128)(4,1)} %bitcast.134), calls=%async_computation.2 | async-start | bytes 8388608
  222.6 7.0 %copy-start.6 = (bf16[512,768]{0,1:T(8,128)(2,1)S(1)}, bf16[512,768]{0,1:T(8,128)(2,1)}, u32[]{:S(2)}) copy-start(bf16[512,768]{0,1:T(8,128)(2,1)} %copy-done.5) | copy-start | bytes 2359300
  229.6 3.0 copy-start.3
  242.5 2.2 copy-start.9
  244.7 2.0 copy-start.17
  244.7 2.0 copy-start.27
  246.7 1.5 copy-start.16
  349.4 6.7 %copy-start.20 = (bf16[96,768]{1,0:T(8,128)(2,1)S(1)}, bf16[96,768]{1,0:T(8,128)(2,1)}, u32[]{:S(2)}) copy-start(bf16[96,768]{1,0:T(8,128)(2,1)} %get-tuple-element.103) | copy-start | bytes 442372
  349.4 7.5 %copy-start.19 = (bf16[96,3072]{1,0:T(8,128)(2,1)S(1)}, bf16[96,3072]{1,0:T(8,128)(2,1)}, u32[]{:S(2)}) copy-start(bf16[96,3072]{1,0:T(8,128)(2,1)} %get-tuple-element.101) | copy-start | bytes 1769476
  352.8 5.2 %copy-start.18 = (bf16[384,768]{1,0:T(8,128)(2,1)S(1)}, bf16[384,768]{1,0:T(8,128)(2,1)}, u32[]{:S(2)}) copy-start(bf16[384,768]{1,0:T(8,128)(2,1)} %get-tuple-element.102) | copy-start | bytes 1769476
  366.0 11.5 %copy-start.13 = (s32[262144]{0:T(1024)S(1)}, s32[262144]{0:T(1024)}, u32[]{:S(2)}) copy-start(s32[262144]{0:T(1024)} %constant.78) | copy-start | bytes 3145732
  377.5 49.9 %copy-start.1 = (f32[32,12]{0,1:T(8,128)S(1)}, f32[32,12]{0,1:T(8,128)}, u32[]{:S(2)}) copy-start(f32[32,12]{0,1:T(8,128)} %param.29) | copy-start | bytes 4612
  (5 other events, 5.7 us)
